TPU v7x, 32 devices: a whole 2x2x4 slice. The times are simulated.
32 devices in a mesh: tm: 4 (over x, core), row: 4 (over z), col: 2 (over y).
Axes of the slice: x: 2, y: 2, z: 4, core: 2. Of those that a mesh axis runs over, the one named last changes fastest.
Arguments:
- records: bfloat16 [192, 2, 16, 2048], P('tm', None, None, ('row', 'col')), may hold values from -6 to 6
- offsets: int32 [8, 8], replicated, may hold values from 0 to 3
Outputs:
- cthree: bfloat16 [2, 16, 2048, 2048], P(None, 'tm', 'row', 'col')
All inputs are finite; a program needn't handle non-finite values.
Results may differ from a plain program's by a relative error of at most 0.017.
Values may be sent and summed in bfloat16 or wider, within the bound.
A program may use at most 192 MiB of HBM per device.

v0:
```python
import math

import jax
import jax.numpy as jnp
from jax import lax
from jax.sharding import PartitionSpec as P

S = 2048
F = 16
BLOCK = 256
NOFF = 4
NB = 8


def lag_kernels(bins, count):
    freq = jnp.arange(bins, dtype=jnp.int32)
    lag = jnp.minimum(freq, bins - freq)
    starts = jnp.arange(count, dtype=jnp.int32)[:, None] + 2
    inside = (lag[None, :] >= starts) & (lag[None, :] < starts + 3)
    weights = jnp.where(inside, jnp.float32(1.0), jnp.float32(0.1))
    phase = (freq[:, None, None] - freq[None, :, None]) * freq[None, None, :] % bins
    cosines = jnp.cos(phase.astype(jnp.float32) * jnp.float32(2.0 * math.pi / bins))
    return jnp.einsum(
        "ot,fgt->ofg", weights, cosines, precision=lax.Precision.HIGHEST
    ) / jnp.float32(bins)


def apply_window(tile, row_first, col_first, offsets, lagged):
    bins = tile.shape[1]
    row_count = tile.shape[2]
    col_count = tile.shape[3]
    col_width = min(BLOCK, col_count)
    row_groups = row_count // BLOCK
    col_groups = col_count // col_width
    row_ids = (row_first + jnp.arange(row_groups, dtype=jnp.int32) * BLOCK) // BLOCK
    col_ids = (col_first + jnp.arange(col_groups, dtype=jnp.int32) * col_width) // BLOCK
    block_ids = jnp.arange(NB, dtype=jnp.int32)
    row_onehot = (row_ids[:, None] == block_ids[None, :]).astype(jnp.float32)
    col_onehot = (col_ids[:, None] == block_ids[None, :]).astype(jnp.float32)
    symmetric = ((offsets + offsets.T) % NOFF).astype(jnp.float32)
    shift_table = jnp.dot(
        jnp.dot(row_onehot, symmetric, precision=lax.Precision.HIGHEST),
        col_onehot.T,
        precision=lax.Precision.HIGHEST,
    )
    kernels = jnp.zeros((row_groups, col_groups, bins, bins), jnp.float32)
    for offset in range(NOFF):
        picked = (shift_table == jnp.float32(offset)).astype(jnp.float32)
        kernels = kernels + picked[:, :, None, None] * lagged[offset][None, None]
    shaped = tile.reshape(2, bins, row_groups, BLOCK, col_groups, col_width)
    result = jnp.einsum("xyfg,cgxayb->cfxayb", kernels, shaped, precision=lax.Precision.HIGHEST)
    return result.reshape(tile.shape).astype(jnp.bfloat16)


def fold_columns(row_band, piece):
    left_real = row_band[0]
    left_imag = row_band[1]
    left_both = jnp.concatenate([left_real, left_imag], axis=2)
    right_real = jnp.concatenate([piece[0], -piece[1]], axis=1)
    right_imag = jnp.concatenate([piece[1], piece[0]], axis=1)
    real_part = jnp.einsum(
        "fak,fkb->fab", left_both, right_real, preferred_element_type=jnp.float32
    )
    imag_part = jnp.einsum(
        "fak,fkb->fab", left_both, right_imag, preferred_element_type=jnp.float32
    )
    return (real_part, imag_part)


def panel_product_each(own_bins):
    row_band = lax.all_gather(own_bins, "col", axis=3, tiled=True)
    real_part, imag_part = fold_columns(
        row_band, lax.all_gather(own_bins, "row", axis=2, tiled=True)
    )
    return (jnp.stack([real_part, imag_part]) / jnp.float32(math.sqrt(S))).astype(jnp.bfloat16)


def tile_terms(left, right, scale):
    left_both = jnp.concatenate([left[:, 0], left[:, 1]], axis=0)
    right_real = jnp.concatenate([right[:, 0], right[:, 1]], axis=0)
    right_imag = jnp.concatenate([right[:, 1], -right[:, 0]], axis=0)
    real_part = jnp.einsum(
        "kfa,kfb->fab", left_both, right_real, preferred_element_type=jnp.float32
    )
    imag_part = jnp.einsum(
        "kfa,kfb->fab", left_both, right_imag, preferred_element_type=jnp.float32
    )
    return jnp.stack([real_part, imag_part]) / scale


def on_device(records, offsets):
    rec_here = records.shape[0]
    time_count = lax.axis_size("tm")
    total_records = rec_here * time_count
    scale = jnp.float32(math.sqrt(total_records))
    whole = lax.all_gather(records, ("row", "col"), axis=3, tiled=True)
    tile_rows = S // lax.axis_size("row")
    tile_cols = S // lax.axis_size("col")
    row_first = lax.axis_index("row") * tile_rows
    col_first = lax.axis_index("col") * tile_cols
    lagged = lag_kernels(F, NOFF)
    bins_here = F // time_count
    left = lax.dynamic_slice_in_dim(whole, row_first, tile_rows, 3)
    right = lax.dynamic_slice_in_dim(whole, col_first, tile_cols, 3)
    partial_gram = tile_terms(left, right, scale)
    summed = lax.psum(partial_gram.astype(jnp.bfloat16), "tm").astype(jnp.float32)
    windowed = apply_window(summed, row_first, col_first, offsets, lagged)
    own_bins = lax.dynamic_slice_in_dim(windowed, lax.axis_index("tm") * bins_here, bins_here, 1)
    pieces = []
    for bin_index in range(bins_here):
        pieces.append(panel_product_each(own_bins[:, bin_index : bin_index + 1]))
    return jnp.concatenate(pieces, axis=1)


def solution(mesh):
    return jax.shard_map(
        on_device,
        mesh=mesh,
        in_specs=(P("tm", None, None, ("row", "col")), P()),
        out_specs=P(None, "tm", "row", "col"),
        check_vma=False,
    )
```

profile of v0, /device:TPU:0, one launch (start us, length us, event | category | flops | bytes accessed | tf_op | source)
XLA Modules:
  0.0 1821.8 jit_solution(11678642230504693142)
XLA Ops:
  9.1 103.0 %all-gather.10.cloned.1.call-done = bf16[48,2,16,2048]{3,0,2,1:T(8,128)(2,1)} async-done(((bf16[48,2,16,256]{3,0,2,1:T(8,128)(2,1)}), bf16[48,2,16,2048]{3,0,2,1:T(8,128)(2,1)}) %all-gather.10.cloned.1.call-update) | async-done | bytes 6291472 | tf_op jit(solution)/shard_map/all_gather | solution.py:96
  117.2 13.3 convolution_bitcast_fusion.1
  130.4 13.1 convolution_bitcast_fusion
  143.5 32.9 %fusion = bf16[2,16,512,1024]{3,2,1,0:T(8,128)(2,1)} fusion(f32[1,16,512,1024]{3,2,1,0:T(8,128)} %convolution_bitcast_fusion, f32[1,16,512,1024]{3,2,1,0:T(8,128)} %convolution_bitcast_fusion.1), kind=kLoop, calls=%fused_computation.1 | loop fusion | flops 50331648 | bytes 100663296 | tf_op jit(solution)/shard_map/convert_element_type | solution.py:106
  176.4 54.7 %reshape.348 = bf16[2,16,2,256,4,256]{5,4,3,2,1,0:T(4,128)(2,1)} reshape(bf16[2,16,512,1024]{3,2,1,0:T(8,128)(2,1)} %fusion) | data formatting | bytes 67108864 | tf_op jit(solution)/shard_map/reshape | solution.py:50
  231.1 31.3 %copy.7 = bf16[2,16,2,256,4,256]{5,1,3,0,4,2:T(8,128)(2,1)} copy(bf16[2,16,2,256,4,256]{5,4,3,2,1,0:T(4,128)(2,1)} %reshape.348) | data formatting | bytes 67108864 | tf_op jit(solution)/shard_map/reshape | solution.py:50
  265.2 553.8 %all-reduce.2.cloned.1.call-done = bf16[2,16,2,256,4,256]{5,1,3,0,4,2:T(8,128)(2,1)} async-done(((bf16[2,16,2,256,4,256]{5,1,3,0,4,2:T(8,128)(2,1)}), bf16[2,16,2,256,4,256]{5,1,3,0,4,2:T(8,128)(2,1)}) %all-reduce.2.cloned.1.call-update) | async-done | bytes 33554448 | tf_op jit(solution)/shard_map/psum | solution.py:106
  819.0 33.3 %convert_bitcast_fusion = bf16[2,16,2,256,4,256]{5,1,3,0,4,2:T(8,128)(2,1)} fusion(bf16[2,16,2,256,4,256]{5,1,3,0,4,2:T(8,128)(2,1)} %all-reduce.2.cloned.1.call-done, f32[16,16]{1,0:T(8,128)S(1)} %bitcast.175, f32[2,4]{1,0:T(2,128)S(1)} %get-tuple-element.34, f32[16,16]{1,0:T(8,128)S(1)} %bitcast.176, f32[2,4]{1,0:T(2,128)S(1)} %get-tuple-element.35, ...), kind=kOutput, calls=%fused_computation.2 | convolution fusion | flops 3238017024 | bytes 67113088 | tf_op jit(solution)/shard_map/xyfg,cgxayb->cfxayb/dot_general | solution.py:51
  852.3 42.7 %copy.9 = bf16[2,16,2,256,4,256]{5,4,3,2,1,0:T(4,128)(2,1)} copy(bf16[2,16,2,256,4,256]{5,1,3,0,4,2:T(8,128)(2,1)} %convert_bitcast_fusion) | data formatting | bytes 67108864 | tf_op jit(solution)/shard_map/convert_element_type | solution.py:52
  894.9 53.7 %convert_element_type.86 = bf16[2,16,512,1024]{3,2,1,0:T(8,128)(2,1)} reshape(bf16[2,16,2,256,4,256]{5,4,3,2,1,0:T(4,128)(2,1)} %copy.9) | data formatting | bytes 67108864 | tf_op jit(solution)/shard_map/convert_element_type | solution.py:52
  948.6 7.6 constant_dynamic-slice_fusion.1
  960.8 52.4 %all-gather.12.cloned.1.call-done = bf16[2,1,512,2048]{3,2,1,0:T(8,128)(2,1)} async-done(((bf16[2,1,512,1024]{3,2,1,0:T(8,128)(2,1)}), bf16[2,1,512,2048]{3,2,1,0:T(8,128)(2,1)}) %all-gather.12.cloned.1.call-update) | async-done | bytes 4194320 | tf_op jit(solution)/shard_map/all_gather | solution.py:71
  1013.2 4.8 slice_bitcast_fusion.15
  1018.1 53.4 %all-gather.16.cloned.1.call-done = bf16[2,1,512,2048]{3,2,1,0:T(8,128)(2,1)} async-done(((bf16[2,1,512,1024]{3,2,1,0:T(8,128)(2,1)}), bf16[2,1,512,2048]{3,2,1,0:T(8,128)(2,1)}) %all-gather.16.cloned.1.call-update) | async-done | bytes 4194320 | tf_op jit(solution)/shard_map/all_gather | solution.py:71
  1071.5 4.8 slice_bitcast_fusion.13
  1076.3 53.4 %all-gather.20.cloned.1.call-done = bf16[2,1,512,2048]{3,2,1,0:T(8,128)(2,1)} async-done(((bf16[2,1,512,1024]{3,2,1,0:T(8,128)(2,1)}), bf16[2,1,512,2048]{3,2,1,0:T(8,128)(2,1)}) %all-gather.20.cloned.1.call-update) | async-done | bytes 4194320 | tf_op jit(solution)/shard_map/all_gather | solution.py:71
  1129.7 4.8 slice_bitcast_fusion.11
  1134.5 53.5 %all-gather.24.cloned.1.call-done = bf16[2,1,512,2048]{3,2,1,0:T(8,128)(2,1)} async-done(((bf16[2,1,512,1024]{3,2,1,0:T(8,128)(2,1)}), bf16[2,1,512,2048]{3,2,1,0:T(8,128)(2,1)}) %all-gather.24.cloned.1.call-update) | async-done | bytes 4194320 | tf_op jit(solution)/shard_map/all_gather | solution.py:71
  1188.0 4.8 slice_bitcast_fusion.9
  1192.8 146.5 %all-gather.14.cloned.1.call-done = bf16[2,1,2048,1024]{3,2,1,0:T(8,128)(2,1)} async-done(((bf16[2,1,512,1024]{3,2,1,0:T(8,128)(2,1)}), bf16[2,1,2048,1024]{3,2,1,0:T(8,128)(2,1)}) %all-gather.14.cloned.1.call-update) | async-done | bytes 8388624 | tf_op jit(solution)/shard_map/all_gather | solution.py:73
  1343.7 145.1 %all-gather.18.cloned.1.call-done = bf16[2,1,2048,1024]{3,2,1,0:T(8,128)(2,1)} async-done(((bf16[2,1,512,1024]{3,2,1,0:T(8,128)(2,1)}), bf16[2,1,2048,1024]{3,2,1,0:T(8,128)(2,1)}) %all-gather.18.cloned.1.call-update) | async-done | bytes 8388624 | tf_op jit(solution)/shard_map/all_gather | solution.py:73
  1493.4 145.0 %all-gather.22.cloned.1.call-done = bf16[2,1,2048,1024]{3,2,1,0:T(8,128)(2,1)} async-done(((bf16[2,1,512,1024]{3,2,1,0:T(8,128)(2,1)}), bf16[2,1,2048,1024]{3,2,1,0:T(8,128)(2,1)}) %all-gather.22.cloned.1.call-update) | async-done | bytes 8388624 | tf_op jit(solution)/shard_map/all_gather | solution.py:73
  1641.0 7.2 slice_bitcast_fusion.6
  1648.4 4.6 slice_bitcast_fusion.4
  1656.6 9.4 fusion.42
  1666.0 10.7 fusion.41
  1676.7 8.9 fusion.40
  1685.5 10.9 fusion.39
  1696.4 5.9 fusion.38
  1702.3 5.9 fusion.37
  1708.2 79.5 %all-gather.26.cloned.1.call-done = bf16[2,1,2048,1024]{3,2,1,0:T(8,128)(2,1)} async-done(((bf16[2,1,512,1024]{3,2,1,0:T(8,128)(2,1)}), bf16[2,1,2048,1024]{3,2,1,0:T(8,128)(2,1)}) %all-gather.26.cloned.1.call-update) | async-done | bytes 8388624 | tf_op jit(solution)/shard_map/all_gather | solution.py:73
  1800.3 4.6 fusion.35
  (86 shorter events, 52.2 us)
Async XLA Ops:
  6.5 105.5 %all-gather.10.cloned.1.call-start = ((), (), s32[]{:S(2)}) async-start(), calls=%async_computation | async-start | bytes 7077888 | tf_op jit(solution)/shard_map/all_gather | solution.py:96
  9.0 810.0 %all-reduce.2.cloned.1.call-start = ((), (), s32[]{:S(2)}) async-start(), calls=%async_computation.1 | async-start | bytes 67108864 | tf_op jit(solution)/shard_map/psum | solution.py:106
  262.5 0.7 copy-start.14
  262.5 750.7 %all-gather.12.cloned.1.call-start = ((), (), s32[]{:S(2)}) async-start(), calls=%async_computation.2 | async-start | bytes 6291456 | tf_op jit(solution)/shard_map/all_gather | solution.py:71
  956.3 115.2 %all-gather.16.cloned.1.call-start = ((), (), s32[]{:S(2)}) async-start(), calls=%async_computation.4 | async-start | bytes 6291456 | tf_op jit(solution)/shard_map/all_gather | solution.py:71
  956.9 172.9 %all-gather.20.cloned.1.call-start = ((), (), s32[]{:S(2)}) async-start(), calls=%async_computation.6 | async-start | bytes 6291456 | tf_op jit(solution)/shard_map/all_gather | solution.py:71
  957.4 230.5 %all-gather.24.cloned.1.call-start = ((), (), s32[]{:S(2)}) async-start(), calls=%async_computation.8 | async-start | bytes 6291456 | tf_op jit(solution)/shard_map/all_gather | solution.py:71
  958.0 381.3 %all-gather.14.cloned.1.call-start = ((), (), s32[]{:S(2)}) async-start(), calls=%async_computation.3 | async-start | bytes 10485760 | tf_op jit(solution)/shard_map/all_gather | solution.py:73
  958.8 530.0 %all-gather.18.cloned.1.call-start = ((), (), s32[]{:S(2)}) async-start(), calls=%async_computation.5 | async-start | bytes 10485760 | tf_op jit(solution)/shard_map/all_gather | solution.py:73
  959.5 678.8 %all-gather.22.cloned.1.call-start = ((), (), s32[]{:S(2)}) async-start(), calls=%async_computation.7 | async-start | bytes 10485760 | tf_op jit(solution)/shard_map/all_gather | solution.py:73
  960.3 827.4 %all-gather.26.cloned.1.call-start = ((), (), s32[]{:S(2)}) async-start(), calls=%async_computation.9 | async-start | bytes 10485760 | tf_op jit(solution)/shard_map/all_gather | solution.py:73
  1638.3 9.8 slice-start
  1641.0 7.5 slice-start.1
  1641.0 12.1 slice-start.2
  1648.4 6.0 slice-start.3
  1654.4 2.2 copy-start.2
  1666.0 10.7 copy-start.1
  1666.0 10.7 copy-start.13
  1685.5 10.9 copy-start.11
  1685.5 10.9 copy-start.12
  1787.7 5.8 copy-start
  1793.5 1.6 copy-start.9
  1793.5 2.2 copy-start.10
  1800.3 4.6 copy-start.3
  1800.3 4.6 copy-start.4
  1804.9 1.6 copy-start.5
  1805.0 2.2 copy-start.6
  1807.2 1.6 copy-start.7
  1807.2 2.2 copy-start.8
Sparse Core Ops, SparseCore 0:
  9.4 102.6 all-gather.9
  262.6 556.3 all-reduce.1
  956.4 56.7 all-gather.11
  1014.7 56.7 all-gather.15
  1073.0 56.7 all-gather.19
  1131.2 56.7 all-gather.23
  1189.6 149.6 all-gather.13
  1341.0 147.8 all-gather.17
  1490.5 147.8 all-gather.21
  1639.8 147.8 all-gather.25
where the time goes:
time: 1830 us; the launch traced here: 1820 us
  waiting for transfers between devices  1390 us (76%)
  local copies, waits for them, and re-layouts  242 us (13%)
  matrix products  122 us (7%)
  other arithmetic  53.1 us (3%)
    psum x1, waiting for transfers between devices, on_device(): lax.psum(partial_gram.astype(jnp.bfloat16), 'tm').astype(jnp.float32)  554 us
    all_gather x4, waiting for transfers between devices, panel_product_each(): lax.all_gather(own_bins, 'row', axis=2, tiled=True)  516 us
    all_gather x4, waiting for transfers between devices, panel_product_each(): row_band = lax.all_gather(own_bins, 'col', axis=3, tiled=True)  213 us
    all_gather x1, waiting for transfers between devices, on_device(): whole = lax.all_gather(records, ('row', 'col'), axis=3, tiled=True)  103 us
    convert_element_type x2, local copies, waits for them, and re-layouts, apply_window(): return result.reshape(tile.shape).astype(jnp.bfloat16)  96.4 us
    reshape x2, local copies, waits for them, and re-layouts, apply_window(): shaped = tile.reshape(2, bins, row_groups, BLOCK, col_groups, col_width)  86 us
  transfers between devices with their start and end apart: 10, of which 10 were waited for; matrix products, arithmetic and copies ran while one was open for 5% of the time, Pallas kernels for 0%

commit v1 on v0

v1 whole, which is shorter than its diff:
```python
import functools
import math

import jax
import jax.numpy as jnp
import numpy as np
from jax import lax
from jax.experimental import pallas as pl
from jax.experimental.pallas import tpu as pltpu
from jax.sharding import PartitionSpec as P

BLOCK = 256
NOFF = 4
SUB = 16


def lag_table(bins):
    freq = np.arange(bins)
    lag = np.minimum(freq, bins - freq)
    starts = np.arange(NOFF)[:, None] + 2
    inside = (lag[None, :] >= starts) & (lag[None, :] < starts + 3)
    weights = np.where(inside, 1.0, 0.1)
    phase = (freq[:, None, None] - freq[None, :, None]) * freq[None, None, :] % bins
    cosines = np.cos(phase * (2.0 * math.pi / bins))
    return np.einsum("ot,fgt->ofg", weights, cosines) / bins


def pair_of(step, core, blocks):
    half = blocks // 2
    main = half * half
    tail = step // main
    row = (step // half) * (1 - tail) + (step - main) * tail
    return core * (half - half // 2 * tail) + row, (step % half) * (1 - tail) + half * tail


def tile_kernel(bins, groups, rec, here, blocks, shift, xa_ref, xb_ref, kmat_ref,
                out_ref, left, gram, tile, mirror, local_sem, send_sem, recv_sem):
    step = pl.program_id(0)
    count = pl.num_programs(0) - 1
    tm = lax.axis_index("tm")
    core = lax.rem(tm, 2)
    partner = tm + 1 - 2 * core
    half = blocks // 2
    deep = groups * 2 * rec
    slot = lax.rem(step, 2)
    a, d = pair_of(jnp.minimum(step, count - 1), core, blocks)
    b = lax.rem(a + d, blocks)

    def copies(at, kind):
        ta, td = pair_of(at, core, blocks)
        tb = lax.rem(ta + td, blocks)
        where = lax.rem(at, 2)
        first, second = (ta, tb) if kind == 0 else (tb, ta)
        rows = pl.ds(pl.multiple_of(first * BLOCK, BLOCK), BLOCK)
        cols = pl.ds(pl.multiple_of(second * BLOCK, BLOCK), BLOCK)
        held = tile if kind == 0 else mirror
        kept = pltpu.make_async_copy(
            held.at[where, pl.ds(core * here, here)], out_ref.at[:, :, rows, cols],
            local_sem.at[kind, where],
        )
        given = pltpu.make_async_remote_copy(
            src_ref=held.at[where, pl.ds((1 - core) * here, here)],
            dst_ref=out_ref.at[:, :, rows, cols],
            send_sem=send_sem.at[kind, where],
            recv_sem=recv_sem.at[kind, at],
            device_id={"tm": partner},
            device_id_type=pl.DeviceIdType.MESH,
        )
        return kept, given

    def begin(at, kind):
        kept, given = copies(at, kind)
        kept.start()
        given.start()

    def finish(at, kind):
        kept, given = copies(at, kind)
        kept.wait()
        given.wait_send()

    def turned(at):
        return pair_of(at, core, blocks)[1] > 0

    @pl.when(step == 0)
    def _():
        barrier = pltpu.get_barrier_semaphore()
        pl.semaphore_signal(
            barrier, inc=1, device_id={"tm": partner}, device_id_type=pl.DeviceIdType.MESH
        )
        pl.semaphore_wait(barrier, 1)

    @pl.when((step < count) & ((d == 0) | (step >= half * half)))
    def _():
        @pl.loop(0, bins)
        def _(g):
            block = xa_ref[:, 0, g]
            crossed = jnp.concatenate([-block[:, rec:], block[:, :rec]], axis=1)
            left[g, :BLOCK] = block.reshape(deep, BLOCK).T
            left[g, BLOCK:] = crossed.reshape(deep, BLOCK).T

    before = jnp.maximum(step - 1, 0)
    old = lax.rem(step + 1, 2)

    @pl.when(step >= 3)
    def _():
        @pl.when(turned(step - 3))
        def _():
            finish(step - 3, 1)

    def gram_of(g):
        both = jnp.dot(
            left[g], xb_ref[:, 0, g].reshape(deep, BLOCK), preferred_element_type=jnp.float32
        ).astype(jnp.bfloat16)
        gram[0, g] = both[:BLOCK]
        gram[1, g] = both[BLOCK:]

    def turn(f):
        mirror[old, f, 0] = tile[old, f, 0].T
        mirror[old, f, 1] = -tile[old, f, 1].T

    per = bins // (2 * here)

    @pl.when(step < count)
    def _():
        @pl.loop(0, 2 * here)
        def _(f):
            for k in range(per):
                gram_of(f * per + k)
            turn(f)

    @pl.when(step == count)
    def _():
        @pl.loop(0, 2 * here)
        def _(f):
            turn(f)

    @pl.when(step >= 1)
    def _():
        @pl.when(turned(before))
        def _():
            begin(before, 1)

    @pl.when(step >= 2)
    def _():
        finish(step - 2, 0)

    @pl.when(step < count)
    def _():
        kernel = kmat_ref[shift[a * blocks + b]]

        @pl.loop(0, BLOCK // SUB // 4)
        def _(quad):
            for k in range(4):
                rows = pl.ds(pl.multiple_of((quad * 4 + k) * SUB, SUB), SUB)
                for c in range(2):
                    part = gram[c, :, rows, :].reshape(bins * SUB, BLOCK)
                    mixed = jnp.dot(kernel, part, preferred_element_type=jnp.float32)
                    tile[slot, :, c, rows, :] = mixed.astype(jnp.bfloat16).reshape(
                        2 * here, SUB, BLOCK
                    )

        begin(step, 0)

    @pl.when(step == count)
    def _():
        finish(count - 1, 0)
        for at in (count - 2, count - 1):
            @pl.when(turned(at))
            def _():
                finish(at, 1)

        @pl.loop(0, count)
        def _(at):
            copies(at, 0)[1].wait_recv()

            @pl.when(turned(at))
            def _():
                copies(at, 1)[1].wait_recv()


def windowed_tiles(spectra, shift, kmat, stations):
    groups, bands, bins, both, width = spectra.shape
    rec = both // 2
    here = bins // groups
    per = width // BLOCK
    blocks = stations // BLOCK
    count = blocks * (blocks + 1) // 4
    block = (groups, 1, bins, both, BLOCK)
    flops = count * bins * 2 * BLOCK * BLOCK * (groups * both * 2 + 4 * here * SUB)

    def pick_a(s, sh):
        a, _ = pair_of(jnp.minimum(s, count - 1), lax.rem(lax.axis_index("tm"), 2), blocks)
        return (0, a // per, 0, 0, lax.rem(a, per))

    def pick_b(s, sh):
        a, d = pair_of(jnp.minimum(s, count - 1), lax.rem(lax.axis_index("tm"), 2), blocks)
        b = lax.rem(a + d, blocks)
        return (0, b // per, 0, 0, lax.rem(b, per))

    return pl.pallas_call(
        functools.partial(tile_kernel, bins, groups, rec, here, blocks),
        out_shape=jax.ShapeDtypeStruct((here, 2, stations, stations), jnp.bfloat16),
        grid_spec=pltpu.PrefetchScalarGridSpec(
            num_scalar_prefetch=1,
            grid=(count + 1,),
            in_specs=[
                pl.BlockSpec(block, pick_a),
                pl.BlockSpec(block, pick_b),
                pl.BlockSpec(kmat.shape, lambda s, sh: (0, 0, 0)),
            ],
            out_specs=pl.BlockSpec(memory_space=pl.ANY),
            scratch_shapes=[
                pltpu.VMEM((bins, 2 * BLOCK, groups * both), jnp.bfloat16),
                pltpu.VMEM((2, bins, BLOCK, BLOCK), jnp.bfloat16),
                pltpu.VMEM((2, 2 * here, 2, BLOCK, BLOCK), jnp.bfloat16),
                pltpu.VMEM((2, 2 * here, 2, BLOCK, BLOCK), jnp.bfloat16),
                pltpu.SemaphoreType.DMA((2, 2)),
                pltpu.SemaphoreType.DMA((2, 2)),
                pltpu.SemaphoreType.DMA((2, count)),
            ],
        ),
        compiler_params=pltpu.CompilerParams(
            vmem_limit_bytes=60 * 2**20, collective_id=0, has_side_effects=True
        ),
        cost_estimate=pl.CostEstimate(flops=flops, bytes_accessed=200 * 2**20, transcendentals=0),
        name="windowed_tiles",
    )(shift, spectra, spectra, kmat)


def square_kernel(scale, place, rows_ref, cols_ref, out_ref):
    left_re = rows_ref[0, 0]
    left_im = rows_ref[0, 1]
    right_re = cols_ref[0, 0]
    right_im = cols_ref[0, 1]
    dot = functools.partial(jnp.dot, preferred_element_type=jnp.float32)
    squares = dot(left_re, right_re)
    crosses = dot(left_im, right_im)
    both = dot(left_re + left_im, right_re + right_im)
    out_ref[0, 0] = ((squares - crosses) * scale).astype(jnp.bfloat16)
    out_ref[1, 0] = ((both - squares - crosses) * scale).astype(jnp.bfloat16)


def square_tiles(windowed, place, tile_rows, tile_cols, scale):
    here, _, stations, _ = windowed.shape
    wide = min(512, tile_cols)
    count = tile_cols // wide
    return pl.pallas_call(
        functools.partial(square_kernel, scale),
        out_shape=jax.ShapeDtypeStruct((2, here, tile_rows, tile_cols), jnp.bfloat16),
        grid_spec=pltpu.PrefetchScalarGridSpec(
            num_scalar_prefetch=1,
            grid=(here, count),
            in_specs=[
                pl.BlockSpec((1, 2, tile_rows, stations), lambda f, j, p: (f, 0, p[0], 0)),
                pl.BlockSpec((1, 2, stations, wide), lambda f, j, p: (f, 0, 0, p[1] * count + j)),
            ],
            out_specs=pl.BlockSpec((2, 1, tile_rows, wide), lambda f, j, p: (0, f, 0, j)),
        ),
        compiler_params=pltpu.CompilerParams(vmem_limit_bytes=56 * 2**20),
        cost_estimate=pl.CostEstimate(
            flops=8 * here * tile_rows * tile_cols * stations,
            bytes_accessed=60 * 2**20,
            transcendentals=0,
        ),
        name="square_tiles",
    )(place, windowed, windowed)


def on_device(mesh, records, offsets):
    rec, _, bins, width = records.shape
    groups = mesh.shape["tm"]
    bands = mesh.shape["row"]
    stations = width * bands * mesh.shape["col"]
    here = bins // groups
    own = jnp.transpose(records, (2, 1, 0, 3)).reshape(bins, 2 * rec, width)
    band = lax.all_gather(own, "col", axis=2, tiled=True)
    spectra = lax.all_gather(band, ("tm", "row"), axis=0)
    spectra = spectra.reshape(groups, bands, bins, 2 * rec, stations // bands)

    chip = lax.axis_index("tm") // 2
    mine = lax.dynamic_slice_in_dim(
        jnp.asarray(lag_table(bins).astype(np.float32)), chip * 2 * here, 2 * here, 1
    )
    kmat = mine[:, :, None, :, None] * jnp.eye(SUB, dtype=jnp.float32)[None, None, :, None, :]
    kmat = kmat.reshape(NOFF, 2 * here * SUB, bins * SUB).astype(jnp.bfloat16)
    shift = ((offsets + offsets.T) % NOFF).reshape(-1)
    windowed = windowed_tiles(spectra, shift, kmat, stations)
    place = jnp.stack([lax.axis_index("row"), lax.axis_index("col")]).astype(jnp.int32)
    scale = 1.0 / (rec * groups * math.sqrt(stations))
    return square_tiles(
        windowed, place, stations // bands, stations // mesh.shape["col"], scale
    )


def solution(mesh):
    return jax.shard_map(
        functools.partial(on_device, mesh),
        mesh=mesh,
        in_specs=(P("tm", None, None, ("row", "col")), P()),
        out_specs=P(None, "tm", "row", "col"),
        check_vma=False,
    )
```

time: 1830 us -> 331 us (0.18)
  waiting for transfers between devices: 1390 us -> 157 us
  local copies, waits for them, and re-layouts: 242 us -> 11 us
  Pallas kernels: 0 us -> 148 us
  matrix products: 122 us -> 0 us
  other arithmetic: 53.1 us -> 2.11 us
    all_gather x9 -> x2, waiting for transfers between devices: 832 us -> 157 us  [the longest x1 127 us: on_device(): spectra = lax.all_gather(band, ('tm', 'row'), axis=0)]
    psum x1 -> x0, waiting for transfers between devices: 554 us -> none  [on_device(): lax.psum(partial_gram.astype(jnp.bfloat16), 'tm').astype(jnp.float32)]
    pallas_call x0 -> x2, Pallas kernels: none -> 148 us  [the longest x1 114 us: windowed_tiles(): pl.pallas_call(functools.partial(tile_kernel, bins, groups, rec, here, bl...]
    dot_general x14 -> x0, matrix products: 122 us -> none  [the longest x1 33.3 us: apply_window(): jnp.einsum('xyfg,cgxayb->cfxayb', kernels, shaped, precision=lax.Precisio...]
    convert_element_type x2 -> x0, local copies, waits for them, and re-layouts: 96.4 us -> none  [apply_window(): return result.reshape(tile.shape).astype(jnp.bfloat16)]
    reshape x2 -> x1, local copies, waits for them, and re-layouts: 86 us -> 0.65 us  [on_device(): shift = ((offsets + offsets.T) % NOFF).reshape(-1)]
    squeeze x10 -> x0, local copies, waits for them, and re-layouts: 39.5 us -> none  [the longest x4 19.2 us: fold_columns(): left_real = row_band[0]]
    convert_element_type x5 -> x2, other arithmetic: 35.3 us -> 0.75 us  [the longest x1 0.75 us: on_device(): kmat = kmat.reshape(NOFF, 2 * here * SUB, bins * SUB).astype(jnp.bfloat16)]
  transfers between devices with their start and end apart: 10 -> 2, of which waited for: 10 -> 2; matrix products, arithmetic and copies ran while one was open for 5% -> 3% of each run, Pallas kernels for 0% -> 0%
where the time goes in v1:
time: 331 us
  waiting for transfers between devices  157 us (47%)
  Pallas kernels  148 us (45%)
  between operations  13.4 us (4%)
  local copies, waits for them, and re-layouts  11 us (3%)
    all_gather x1, waiting for transfers between devices, on_device(): spectra = lax.all_gather(band, ('tm', 'row'), axis=0)  127 us
    pallas_call x1, Pallas kernels, windowed_tiles(): pl.pallas_call(functools.partial(tile_kernel, bins, groups, rec, here, bl...  114 us
    pallas_call x1, Pallas kernels, square_tiles(): pl.pallas_call(functools.partial(square_kernel, scale), out_shape=jax.Sha...  33.9 us
    all_gather x1, waiting for transfers between devices, on_device(): band = lax.all_gather(own, 'col', axis=2, tiled=True)  30 us
  transfers between devices with their start and end apart: 2, of which 2 were waited for; matrix products, arithmetic and copies ran while one was open for 3% of the time, Pallas kernels for 0%

profile of v1, /device:TPU:0, one launch (start us, length us, event | category | flops | bytes accessed | tf_op | source)
XLA Modules:
  0.0 331.1 jit_solution(11872013822179587218)
XLA Ops:
  6.5 0.0 all-gather.4.cloned.1.call-start
  6.5 2.4 copy.8
  9.0 0.0 all-gather.4.cloned.1.call-update
  9.0 0.0 all-gather.6.cloned.1.call-start
  9.1 30.0 %all-gather.4.cloned.1.call-done = bf16[16,96,512]{2,1,0:T(8,128)(2,1)} async-done(((bf16[16,96,256]{2,1,0:T(8,128)(2,1)}), bf16[16,96,512]{2,1,0:T(8,128)(2,1)}) %all-gather.4.cloned.1.call-update) | async-done | bytes 1572880 | tf_op jit(solution)/shard_map/all_gather | solution.py:276
  39.0 0.0 all-gather.6.cloned.1.call-update
  39.1 0.8 copy.7
  39.8 0.7 add_select_fusion
  40.5 0.6 reshape.21.shift
  41.2 0.1 mul.27
  41.3 0.4 mul.28
  41.7 0.7 constant_dynamic-slice_fusion
  42.4 2.4 mul.25
  44.8 3.5 %mul.26 = f32[4,128,256]{2,1,0:T(8,128)S(1)} reshape(f32[4,8,16,16,16]{4,3,2,1,0:T(8,128)} %mul.25) | data formatting | bytes 1048576 | tf_op jit(solution)/shard_map/mul | solution.py:284
  48.3 0.7 pad_add_fusion.place
  49.0 0.7 multiply_convert_fusion.kmat_ref
  49.7 126.7 %all-gather.6.cloned.1.call-done = bf16[256,96,512]{2,1,0:T(8,128)(2,1)} async-done(((bf16[16,96,512]{2,1,0:T(8,128)(2,1)}), bf16[256,96,512]{2,1,0:T(8,128)(2,1)}) %all-gather.6.cloned.1.call-update) | async-done | bytes 25165840 | tf_op jit(solution)/shard_map/all_gather | solution.py:277
  176.4 114.0 %windowed_tiles.1.rows_ref.cols_ref = bf16[4,2,2048,2048]{3,2,1,0:T(8,128)(2,1)} custom-call(s32[64]{0:T(128)} %reshape.21.shift, bf16[4,4,16,96,512]{4,3,2,1,0:T(8,128)(2,1)} %bitcast.17, bf16[4,4,16,96,512]{4,3,2,1,0:T(8,128)(2,1)} %bitcast.18, bf16[4,128,256]{2,1,0:T(8,128)(2,1)} %multiply_convert_fusion.kmat_ref), custom_call_target="tpu_custom_call" | custom-call | flops 38654705664 | bytes 209715200 | tf_op jit(solution)/shard_map/windowed_tiles/pallas_call | solution.py:200
  290.4 33.9 %square_tiles.1 = bf16[2,4,512,1024]{3,2,1,0:T(8,128)(2,1)} custom-call(s32[2]{0:T(128)} %pad_add_fusion.place, bf16[4,2,2048,2048]{3,2,1,0:T(8,128)(2,1)} %windowed_tiles.1.rows_ref.cols_ref, bf16[4,2,2048,2048]{3,2,1,0:T(8,128)(2,1)} %windowed_tiles.1.rows_ref.cols_ref), custom_call_target="tpu_custom_call" | custom-call | flops 34359738368 | bytes 62914560 | tf_op jit(solution)/shard_map/square_tiles/pallas_call | solution.py:247
  (1 shorter events, 0.0 us)
Async XLA Ops:
  6.5 32.5 %all-gather.4.cloned.1.call-start = ((), (), s32[]{:S(2)}) async-start(), calls=%async_computation | async-start | bytes 2359296 | tf_op jit(solution)/shard_map/all_gather | solution.py:276
  9.0 167.4 %all-gather.6.cloned.1.call-start = ((), (), s32[]{:S(2)}) async-start(), calls=%async_computation.1 | async-start | bytes 26738688 | tf_op jit(solution)/shard_map/all_gather | solution.py:277
Sparse Core Ops, SparseCore 0:
  9.1 29.8 all-gather.3
  40.6 135.7 all-gather.5

commit v2 on v1

--- a/solution.py
+++ b/solution.py
@@ -23,6 +23,133 @@
     phase = (freq[:, None, None] - freq[None, :, None]) * freq[None, None, :] % bins
     cosines = np.cos(phase * (2.0 * math.pi / bins))
     return np.einsum("ot,fgt->ofg", weights, cosines) / bins
+
+
+def gather_kernel(groups, bands, cols, own_ref, out_ref, local_sem, send_sem, recv_sem):
+    tm = lax.axis_index("tm")
+    row = lax.axis_index("row")
+    col = lax.axis_index("col")
+    core = lax.rem(tm, 2)
+    partner = tm + 1 - 2 * core
+    both = own_ref.shape[0]
+    half = both // 2
+    bits = (bands - 1).bit_length()
+
+    def other_row(k):
+        total = 0
+        for bit in range(bits):
+            own_bit = lax.rem(row // 2**bit, 2)
+            total = total + 2**bit * lax.rem(own_bit + k // 2**bit % 2, 2)
+        return total
+
+    chips = [lax.rem(tm + 2 * k, groups) for k in range(1, groups // 2)]
+    columns = [lax.rem(col + k, cols) for k in range(1, cols)]
+    rows = [other_row(k) for k in range(1, bands)]
+
+    barrier = pltpu.get_barrier_semaphore()
+    friends = (
+        [{"tm": t} for t in chips] + [{"col": q} for q in columns]
+        + [{"row": r} for r in rows] + [{"tm": partner}]
+    )
+    for friend in friends:
+        pl.semaphore_signal(
+            barrier, inc=1, device_id=friend, device_id_type=pl.DeviceIdType.MESH
+        )
+    pl.semaphore_wait(barrier, len(friends))
+
+    started = []
+
+    def place(t, r, q):
+        return out_ref.at[t, r * cols + q]
+
+    def copy(t, r, q, target, part, source=None):
+        source = place(t, r, q) if source is None else source
+        target_ref = place(t, r, q)
+        if part is not None:
+            source = source.at[pl.ds(part * half, half)]
+            target_ref = target_ref.at[pl.ds(part * half, half)]
+        return pltpu.make_async_remote_copy(
+            src_ref=source, dst_ref=target_ref,
+            send_sem=send_sem.at[len(started)],
+            recv_sem=recv_sem.at[part or 0, t, r * cols + q],
+            device_id=target, device_id_type=pl.DeviceIdType.MESH,
+        )
+
+    def send(t, r, q, target, part=None, source=None):
+        one = copy(t, r, q, target, part, source)
+        one.start()
+        started.append(one)
+
+    def arrive(t, r, q, part=None):
+        piece = place(t, r, q)
+        if part is not None:
+            piece = piece.at[pl.ds(part * half, half)]
+        pltpu.make_async_copy(piece, piece, recv_sem.at[part or 0, t, r * cols + q]).wait()
+
+    def spread(r, source=None):
+        for t in chips:
+            send(tm, r, col, {"tm": t}, source=source)
+        for q in columns:
+            send(tm, r, col, {"col": q}, source=source)
+        send(tm, r, col, {"tm": partner}, source=source)
+
+    def pass_on(r):
+        for t in chips:
+            arrive(t, r, col)
+            for q in columns:
+                send(t, r, col, {"col": q}, 0)
+            send(t, r, col, {"tm": partner})
+        for q in columns:
+            arrive(tm, r, q)
+            for t in chips:
+                send(tm, r, q, {"tm": t}, 1)
+            send(tm, r, q, {"tm": partner})
+
+    mine = pltpu.make_async_copy(own_ref, place(tm, row, col), local_sem)
+    mine.start()
+    for r in rows:
+        send(tm, row, col, {"row": r}, source=own_ref)
+    spread(row, own_ref)
+    waiting = [row]
+    for r in rows:
+        arrive(tm, r, col)
+        spread(r)
+        pass_on(waiting.pop())
+        waiting.append(r)
+    pass_on(waiting.pop())
+    for r in [row] + rows:
+        for t in chips:
+            for q in columns:
+                arrive(t, r, q, 0)
+                arrive(t, r, q, 1)
+                send(t, r, q, {"tm": partner})
+    for chip in range(groups // 2):
+        t = lax.rem(partner + 2 * chip, groups)
+        for k in range(bands * cols):
+            arrive(t, k // cols, k % cols)
+    mine.wait()
+    for one in started:
+        one.wait_send()
+
+
+def gather_pieces(own, groups, bands, cols):
+    chips = groups // 2
+    sends = (bands - 1) + bands * (chips - 1 + cols - 1 + 1)
+    sends += bands * ((chips - 1) * cols + (cols - 1) * chips + (chips - 1) * (cols - 1))
+    return pl.pallas_call(
+        functools.partial(gather_kernel, groups, bands, cols),
+        out_shape=jax.ShapeDtypeStruct((groups, bands * cols) + own.shape, own.dtype),
+        in_specs=[pl.BlockSpec(memory_space=pl.ANY)],
+        out_specs=pl.BlockSpec(memory_space=pl.ANY),
+        scratch_shapes=[
+            pltpu.SemaphoreType.DMA,
+            pltpu.SemaphoreType.DMA((sends,)),
+            pltpu.SemaphoreType.DMA((2, groups, bands * cols)),
+        ],
+        compiler_params=pltpu.CompilerParams(collective_id=1, has_side_effects=True),
+        cost_estimate=pl.CostEstimate(flops=0, bytes_accessed=50 * 2**20, transcendentals=0),
+        name="gather_pieces",
+    )(own)
 
 
 def pair_of(step, core, blocks):
@@ -273,9 +400,12 @@
     stations = width * bands * mesh.shape["col"]
     here = bins // groups
     own = jnp.transpose(records, (2, 1, 0, 3)).reshape(bins, 2 * rec, width)
-    band = lax.all_gather(own, "col", axis=2, tiled=True)
-    spectra = lax.all_gather(band, ("tm", "row"), axis=0)
-    spectra = spectra.reshape(groups, bands, bins, 2 * rec, stations // bands)
+    if width == BLOCK:
+        spectra = gather_pieces(own, groups, bands, mesh.shape["col"])
+    else:
+        band = lax.all_gather(own, "col", axis=2, tiled=True)
+        spectra = lax.all_gather(band, ("tm", "row"), axis=0)
+        spectra = spectra.reshape(groups, bands, bins, 2 * rec, stations // bands)
 
     chip = lax.axis_index("tm") // 2
     mine = lax.dynamic_slice_in_dim(

time: 331 us -> 291 us (0.88)
  waiting for transfers between devices: 157 us -> 0 us
  Pallas kernels: 148 us -> 277 us
  between operations: 13.4 us -> 0.04 us
    all_gather x2 -> x0, waiting for transfers between devices: 157 us -> none  [the longest x1 127 us: on_device(): spectra = lax.all_gather(band, ('tm', 'row'), axis=0)]
    pallas_call x0 -> x1, Pallas kernels: none -> 130 us  [gather_pieces(): pl.pallas_call(functools.partial(gather_kernel, groups, bands, cols), out...]
  transfers between devices with their start and end apart: 2 -> 0, of which waited for: 2 -> 0; matrix products, arithmetic and copies ran while one was open for 3% -> 0% of each run, Pallas kernels for 0% -> 0%
where the time goes in v2:
time: 291 us; the launch traced here: 290 us
  Pallas kernels  277 us (95%)
  local copies, waits for them, and re-layouts  10.9 us (4%)
    pallas_call x1, Pallas kernels, gather_pieces(): pl.pallas_call(functools.partial(gather_kernel, groups, bands, cols), out...  130 us
    pallas_call x1, Pallas kernels, windowed_tiles(): pl.pallas_call(functools.partial(tile_kernel, bins, groups, rec, here, bl...  113 us
    pallas_call x1, Pallas kernels, square_tiles(): pl.pallas_call(functools.partial(square_kernel, scale), out_shape=jax.Sha...  33.9 us
    mul x4, local copies, waits for them, and re-layouts, on_device(): mine[:, :, None, :, None]  6.35 us

profile of v2, /device:TPU:0, one launch (start us, length us, event | category | flops | bytes accessed | tf_op | source)
XLA Modules:
  0.0 290.3 jit_solution(7085775678451584898)
XLA Ops:
  0.0 0.6 pad_add_fusion.place
  0.6 0.8 copy.4
  1.4 0.7 add_select_fusion
  2.1 0.6 reshape.18.shift
  2.7 0.7 constant_dynamic-slice_fusion
  3.4 2.4 copy.5
  5.9 0.1 mul.27
  6.0 0.4 mul.28
  6.4 2.4 mul.25
  8.8 3.5 %mul.26 = f32[4,128,256]{2,1,0:T(8,128)S(1)} reshape(f32[4,8,16,16,16]{4,3,2,1,0:T(8,128)} %mul.25) | data formatting | bytes 1048576 | tf_op jit(solution)/shard_map/mul | solution.py:414
  12.2 0.7 multiply_convert_fusion.kmat_ref
  13.0 130.1 %gather_pieces.1.xa_ref.xb_ref = bf16[4,8,16,96,256]{4,3,2,1,0:T(8,128)(2,1)} custom-call(bf16[16,96,256]{2,1,0:T(8,128)(2,1)} %bitcast.14), custom_call_target="tpu_custom_call" | custom-call | bytes 52428800 | tf_op jit(solution)/shard_map/gather_pieces/pallas_call | solution.py:139
  143.1 113.3 %windowed_tiles.1.rows_ref.cols_ref = bf16[4,2,2048,2048]{3,2,1,0:T(8,128)(2,1)} custom-call(s32[64]{0:T(128)} %reshape.18.shift, bf16[4,8,16,96,256]{4,3,2,1,0:T(8,128)(2,1)} %gather_pieces.1.xa_ref.xb_ref, bf16[4,8,16,96,256]{4,3,2,1,0:T(8,128)(2,1)} %gather_pieces.1.xa_ref.xb_ref, bf16[4,128,256]{2,1,0:T(8,128)(2,1)} %multiply_convert_fusion.kmat_ref), custom_call_target="tpu_custom_call" | custom-call | flops 38654705664 | bytes 209715200 | tf_op jit(solution)/shard_map/windowed_tiles/pallas_call | solution.py:327
  256.4 33.9 %square_tiles.1 = bf16[2,4,512,1024]{3,2,1,0:T(8,128)(2,1)} custom-call(s32[2]{0:T(128)} %pad_add_fusion.place, bf16[4,2,2048,2048]{3,2,1,0:T(8,128)(2,1)} %windowed_tiles.1.rows_ref.cols_ref, bf16[4,2,2048,2048]{3,2,1,0:T(8,128)(2,1)} %windowed_tiles.1.rows_ref.cols_ref), custom_call_target="tpu_custom_call" | custom-call | flops 34359738368 | bytes 62914560 | tf_op jit(solution)/shard_map/square_tiles/pallas_call | solution.py:374
  (1 shorter events, 0.0 us)

commit v3 on v1

--- a/solution.py
+++ b/solution.py
@@ -227,6 +227,345 @@
     )(shift, spectra, spectra, kmat)
 
 
+def fused_kernel(groups, bands, cols, bins, rec, here, shift, own_ref, kmat_ref, out_ref,
+                 held, left, gram, tile, mirror, own_sem, piece_send, piece_recv,
+                 local_sem, send_sem, recv_sem):
+    step = pl.program_id(0)
+    count = pl.num_programs(0) - 1
+    tm = lax.axis_index("tm")
+    row = lax.axis_index("row")
+    col = lax.axis_index("col")
+    core = lax.rem(tm, 2)
+    partner = tm + 1 - 2 * core
+    blocks = bands * cols
+    deep = groups * 2 * rec
+    slot = lax.rem(step, 2)
+    old = lax.rem(step + 1, 2)
+    mesh_id = pl.DeviceIdType.MESH
+    chip = lax.rem(tm + 2, groups)
+    side = lax.rem(col + 1, cols)
+    bin_half = bins // 2
+    arrival = [(0, 0), (1, 0), (0, 1), (2, 0), (1, 1), (3, 0), (2, 1), (3, 1)]
+
+    def row_at(k):
+        low = lax.rem(lax.rem(row, 2) + k % 2, 2)
+        high = lax.rem(row // 2 + k // 2, 2)
+        return 2 * high + low
+
+    def block_at(n):
+        total = 0
+        for index, (k, other) in enumerate(arrival):
+            where = row_at(k) * cols + (side if other else col)
+            total = total + jnp.where(n == index, where, 0)
+        return total
+
+    def pair(at, who):
+        t = 2 * at + who
+        n = 0
+        for index in range(1, blocks):
+            n = n + jnp.minimum(t // (index * (index + 1) // 2), 1)
+        return n, t - n * (n + 1) // 2
+
+    def send(index, t, k, q, target, part=None, source=None):
+        block = row_at(k) * cols + q
+        there = held.at[t, block]
+        source = there if source is None else source
+        if part is not None:
+            source = source.at[pl.ds(part * bin_half, bin_half)]
+            there = there.at[pl.ds(part * bin_half, bin_half)]
+        return pltpu.make_async_remote_copy(
+            src_ref=source, dst_ref=there, send_sem=piece_send.at[index],
+            recv_sem=piece_recv.at[part or 0, t, block], device_id=target, device_id_type=mesh_id,
+        )
+
+    def arrive(t, k, q, part=None):
+        block = row_at(k) * cols + q
+        piece = held.at[t, block]
+        if part is not None:
+            piece = piece.at[pl.ds(part * bin_half, bin_half)]
+        pltpu.make_async_copy(piece, piece, piece_recv.at[part or 0, t, block]).wait()
+
+    def own_sends():
+        return [send(k - 1, tm, 0, col, {"row": row_at(k)}, source=own_ref) for k in (1, 2, 3)]
+
+    def spread(k):
+        source = own_ref if k == 0 else None
+        base = 3 + 8 * k
+        return [
+            send(base, tm, k, col, {"tm": chip}, source=source),
+            send(base + 1, tm, k, col, {"col": side}, source=source),
+            send(base + 2, tm, k, col, {"tm": partner}, source=source),
+        ]
+
+    def pass_chip(k):
+        base = 6 + 8 * k
+        return [
+            send(base, chip, k, col, {"col": side}, 0),
+            send(base + 1, chip, k, col, {"tm": partner}),
+        ]
+
+    def pass_side(k):
+        base = 8 + 8 * k
+        return [
+            send(base, tm, k, side, {"tm": chip}, 1),
+            send(base + 1, tm, k, side, {"tm": partner}),
+        ]
+
+    def pass_corner(k):
+        return [send(10 + 8 * k, chip, k, side, {"tm": partner})]
+
+    def start(copies):
+        for one in copies:
+            one.start()
+
+    def row_piece(k):
+        arrive(tm, k, col)
+        start(spread(k))
+
+    def edge_pieces(k):
+        arrive(chip, k, col)
+        start(pass_chip(k))
+        arrive(tm, k, side)
+        start(pass_side(k))
+
+    def corner_piece(k):
+        arrive(chip, k, side, 0)
+        arrive(chip, k, side, 1)
+        start(pass_corner(k))
+
+    def from_core(k, q):
+        arrive(partner, k, q)
+        arrive(lax.rem(partner + 2, groups), k, q)
+
+    mine = pltpu.make_async_copy(own_ref, held.at[tm, row * cols + col], own_sem)
+
+    @pl.when(step == 0)
+    def _():
+        barrier = pltpu.get_barrier_semaphore()
+        friends = [{"tm": chip}, {"col": side}, {"tm": partner}]
+        friends += [{"row": row_at(k)} for k in (1, 2, 3)]
+        for friend in friends:
+            pl.semaphore_signal(barrier, inc=1, device_id=friend, device_id_type=mesh_id)
+        pl.semaphore_wait(barrier, len(friends))
+        first, second, third = own_sends()
+        first.start()
+        start(spread(0))
+        second.start()
+        mine.start()
+        row_piece(1)
+        third.start()
+        edge_pieces(0)
+        mine.wait()
+        edge_pieces(1)
+        from_core(0, col)
+        from_core(1, col)
+
+    @pl.when(step == 1)
+    def _():
+        row_piece(2)
+        corner_piece(0)
+        from_core(0, side)
+
+    @pl.when(step == 3)
+    def _():
+        row_piece(3)
+        edge_pieces(2)
+        from_core(2, col)
+
+    @pl.when(step == 5)
+    def _():
+        corner_piece(1)
+        from_core(1, side)
+
+    @pl.when(step == 7)
+    def _():
+        edge_pieces(3)
+        from_core(3, col)
+
+    @pl.when(step == 10)
+    def _():
+        corner_piece(2)
+        from_core(2, side)
+
+    @pl.when(step == 14)
+    def _():
+        corner_piece(3)
+        from_core(3, side)
+
+    now = jnp.minimum(step, count - 1)
+    n, m = pair(now, core)
+    a = block_at(n)
+    b = block_at(m)
+    before = jnp.maximum(step - 1, 0)
+
+    def copies(at, kind, who):
+        tn, tk = pair(at, who)
+        first, second = (tn, tk) if kind == 0 else (tk, tn)
+        where = lax.rem(at, 2)
+        rows = pl.ds(pl.multiple_of(block_at(first) * BLOCK, BLOCK), BLOCK)
+        columns = pl.ds(pl.multiple_of(block_at(second) * BLOCK, BLOCK), BLOCK)
+        source = tile if kind == 0 else mirror
+        kept = pltpu.make_async_copy(
+            source.at[where, pl.ds(core * here, here)], out_ref.at[:, :, rows, columns],
+            local_sem.at[kind, where],
+        )
+        given = pltpu.make_async_remote_copy(
+            src_ref=source.at[where, pl.ds((1 - core) * here, here)],
+            dst_ref=out_ref.at[:, :, rows, columns],
+            send_sem=send_sem.at[kind, where],
+            recv_sem=recv_sem.at[kind, at],
+            device_id={"tm": partner},
+            device_id_type=mesh_id,
+        )
+        return kept, given
+
+    def begin(at, kind):
+        kept, given = copies(at, kind, core)
+        kept.start()
+        given.start()
+
+    def finish(at, kind):
+        kept, given = copies(at, kind, core)
+        kept.wait()
+        given.wait_send()
+
+    def turned(at, who):
+        tn, tk = pair(at, who)
+        return tn != tk
+
+    @pl.when((step < count) & ((step == 0) | (n != pair(before, core)[0])))
+    def _():
+        @pl.loop(0, bins)
+        def _(g):
+            block = held[:, a, g]
+            crossed = jnp.concatenate([-block[:, rec:], block[:, :rec]], axis=1)
+            left[g, :BLOCK] = block.reshape(deep, BLOCK).T
+            left[g, BLOCK:] = crossed.reshape(deep, BLOCK).T
+
+    @pl.when(step >= 3)
+    def _():
+        @pl.when(turned(step - 3, core))
+        def _():
+            finish(step - 3, 1)
+
+    def gram_of(g):
+        both = jnp.dot(
+            left[g], held[:, b, g].reshape(deep, BLOCK), preferred_element_type=jnp.float32
+        ).astype(jnp.bfloat16)
+        gram[0, g] = both[:BLOCK]
+        gram[1, g] = both[BLOCK:]
+
+    def turn(f):
+        mirror[old, f, 0] = tile[old, f, 0].T
+        mirror[old, f, 1] = -tile[old, f, 1].T
+
+    per = bins // (2 * here)
+
+    @pl.when(step < count)
+    def _():
+        @pl.loop(0, 2 * here)
+        def _(f):
+            for k in range(per):
+                gram_of(f * per + k)
+            turn(f)
+
+    @pl.when(step == count)
+    def _():
+        @pl.loop(0, 2 * here)
+        def _(f):
+            turn(f)
+
+    @pl.when(step >= 1)
+    def _():
+        @pl.when(turned(before, core))
+        def _():
+            begin(before, 1)
+
+    @pl.when(step >= 2)
+    def _():
+        finish(step - 2, 0)
+
+    @pl.when(step < count)
+    def _():
+        kernel = kmat_ref[0, shift[a * blocks + b]]
+
+        @pl.loop(0, BLOCK // SUB // 4)
+        def _(quad):
+            for k in range(4):
+                rows = pl.ds(pl.multiple_of((quad * 4 + k) * SUB, SUB), SUB)
+                for c in range(2):
+                    part = gram[c, :, rows, :].reshape(bins * SUB, BLOCK)
+                    mixed = jnp.dot(kernel, part, preferred_element_type=jnp.float32)
+                    tile[slot, :, c, rows, :] = mixed.astype(jnp.bfloat16).reshape(
+                        2 * here, SUB, BLOCK
+                    )
+
+        begin(step, 0)
+
+    @pl.when(step == count)
+    def _():
+        finish(count - 1, 0)
+        for at in (count - 2, count - 1):
+            @pl.when(turned(at, core))
+            def _():
+                finish(at, 1)
+
+        @pl.loop(0, count)
+        def _(at):
+            copies(at, 0, 1 - core)[1].wait_recv()
+
+            @pl.when(turned(at, 1 - core))
+            def _():
+                copies(at, 1, 1 - core)[1].wait_recv()
+
+        for one in own_sends():
+            one.wait_send()
+        for k in range(bands):
+            for one in spread(k) + pass_chip(k) + pass_side(k) + pass_corner(k):
+                one.wait_send()
+
+
+def fused_tiles(own, shift, kmats, groups, bands, cols, stations):
+    bins, both, _ = own.shape
+    here = bins // groups
+    blocks = bands * cols
+    count = blocks * (blocks + 1) // 4
+    flops = count * bins * 2 * BLOCK * BLOCK * (groups * both * 2 + 4 * here * SUB)
+    return pl.pallas_call(
+        functools.partial(fused_kernel, groups, bands, cols, bins, both // 2, here),
+        out_shape=jax.ShapeDtypeStruct((here, 2, stations, stations), jnp.bfloat16),
+        grid_spec=pltpu.PrefetchScalarGridSpec(
+            num_scalar_prefetch=1,
+            grid=(count + 1,),
+            in_specs=[
+                pl.BlockSpec(memory_space=pl.ANY),
+                pl.BlockSpec(
+                    (1,) + kmats.shape[1:], lambda s, sh: (lax.axis_index("tm") // 2, 0, 0, 0)
+                ),
+            ],
+            out_specs=pl.BlockSpec(memory_space=pl.ANY),
+            scratch_shapes=[
+                pltpu.VMEM((groups, blocks) + own.shape, jnp.bfloat16),
+                pltpu.VMEM((bins, 2 * BLOCK, groups * both), jnp.bfloat16),
+                pltpu.VMEM((2, bins, BLOCK, BLOCK), jnp.bfloat16),
+                pltpu.VMEM((2, 2 * here, 2, BLOCK, BLOCK), jnp.bfloat16),
+                pltpu.VMEM((2, 2 * here, 2, BLOCK, BLOCK), jnp.bfloat16),
+                pltpu.SemaphoreType.DMA,
+                pltpu.SemaphoreType.DMA((3 + 8 * bands,)),
+                pltpu.SemaphoreType.DMA((2, groups, blocks)),
+                pltpu.SemaphoreType.DMA((2, 2)),
+                pltpu.SemaphoreType.DMA((2, 2)),
+                pltpu.SemaphoreType.DMA((2, count)),
+            ],
+        ),
+        compiler_params=pltpu.CompilerParams(
+            vmem_limit_bytes=62 * 2**20, collective_id=1, has_side_effects=True
+        ),
+        cost_estimate=pl.CostEstimate(flops=flops, bytes_accessed=100 * 2**20, transcendentals=0),
+        name="fused_tiles",
+    )(shift, own, kmats)
+
+
 def square_kernel(scale, place, rows_ref, cols_ref, out_ref):
     left_re = rows_ref[0, 0]
     left_im = rows_ref[0, 1]
@@ -273,18 +612,19 @@
     stations = width * bands * mesh.shape["col"]
     here = bins // groups
     own = jnp.transpose(records, (2, 1, 0, 3)).reshape(bins, 2 * rec, width)
-    band = lax.all_gather(own, "col", axis=2, tiled=True)
-    spectra = lax.all_gather(band, ("tm", "row"), axis=0)
-    spectra = spectra.reshape(groups, bands, bins, 2 * rec, stations // bands)
-
-    chip = lax.axis_index("tm") // 2
-    mine = lax.dynamic_slice_in_dim(
-        jnp.asarray(lag_table(bins).astype(np.float32)), chip * 2 * here, 2 * here, 1
-    )
-    kmat = mine[:, :, None, :, None] * jnp.eye(SUB, dtype=jnp.float32)[None, None, :, None, :]
-    kmat = kmat.reshape(NOFF, 2 * here * SUB, bins * SUB).astype(jnp.bfloat16)
+    cols = mesh.shape["col"]
+    table = np.einsum("ofg,st->ofsgt", lag_table(bins), np.eye(SUB))
+    table = table.reshape(NOFF, groups // 2, 2 * here * SUB, bins * SUB)
+    kmats = jnp.asarray(np.moveaxis(table, 1, 0).astype(jnp.bfloat16))
     shift = ((offsets + offsets.T) % NOFF).reshape(-1)
-    windowed = windowed_tiles(spectra, shift, kmat, stations)
+    if width == BLOCK and (groups, bands, cols) == (4, 4, 2):
+        windowed = fused_tiles(own, shift, kmats, groups, bands, cols, stations)
+    else:
+        band = lax.all_gather(own, "col", axis=2, tiled=True)
+        spectra = lax.all_gather(band, ("tm", "row"), axis=0)
+        spectra = spectra.reshape(groups, bands, bins, 2 * rec, stations // bands)
+        kmat = lax.dynamic_index_in_dim(kmats, lax.axis_index("tm") // 2, 0, keepdims=False)
+        windowed = windowed_tiles(spectra, shift, kmat, stations)
     place = jnp.stack([lax.axis_index("row"), lax.axis_index("col")]).astype(jnp.int32)
     scale = 1.0 / (rec * groups * math.sqrt(stations))
     return square_tiles(

time: 331 us -> 243 us (0.73)
  waiting for transfers between devices: 157 us -> 0 us
  Pallas kernels: 148 us -> 238 us
  between operations: 13.4 us -> 0.01 us
  local copies, waits for them, and re-layouts: 11 us -> 3.87 us
    all_gather x2 -> x0, waiting for transfers between devices: 157 us -> none  [the longest x1 127 us: on_device(): spectra = lax.all_gather(band, ('tm', 'row'), axis=0)]
    pallas_call x1, Pallas kernels: 114 us -> 204 us  [fused_tiles(): pl.pallas_call(functools.partial(fused_kernel, groups, bands, cols, bins,...]
    mul x4 -> x0, local copies, waits for them, and re-layouts: 6.38 us -> none  [on_device(): mine[:, :, None, :, None]]
  transfers between devices with their start and end apart: 2 -> 0, of which waited for: 2 -> 0; matrix products, arithmetic and copies ran while one was open for 3% -> 0% of each run, Pallas kernels for 0% -> 0%
where the time goes in v3:
time: 243 us
  Pallas kernels  238 us (98%)
  local copies, waits for them, and re-layouts  3.87 us (2%)
    pallas_call x1, Pallas kernels, fused_tiles(): pl.pallas_call(functools.partial(fused_kernel, groups, bands, cols, bins,...  204 us
    pallas_call x1, Pallas kernels, square_tiles(): pl.pallas_call(functools.partial(square_kernel, scale), out_shape=jax.Sha...  33.9 us

profile of v3, /device:TPU:0, one launch (start us, length us, event | category | flops | bytes accessed | tf_op | source)
XLA Modules:
  0.0 242.7 jit_solution(14651837129475050088)
XLA Ops:
  0.0 0.6 pad_add_fusion.place
  0.6 0.8 copy.4
  1.3 0.7 add_select_fusion
  2.0 0.7 reshape.6.shift
  2.7 2.4 %copy.5 = bf16[16,2,48,256]{3,2,1,0:T(8,128)(2,1)} copy(bf16[16,2,48,256]{3,0,1,2:T(8,128)(2,1)} %bitcast.10) | data formatting | bytes 1572864 | tf_op jit(solution)/shard_map/transpose | solution.py:614
  5.1 203.6 %fused_tiles.1.rows_ref.cols_ref = bf16[4,2,2048,2048]{3,2,1,0:T(8,128)(2,1)} custom-call(s32[64]{0:T(128)} %reshape.6.shift, bf16[16,96,256]{2,1,0:T(8,128)(2,1)} %bitcast.11, bf16[2,4,128,256]{3,2,1,0:T(8,128)(2,1)} %constant.25.clone.kmat_ref), custom_call_target="tpu_custom_call" | custom-call | flops 38654705664 | bytes 104857600 | tf_op jit(solution)/shard_map/fused_tiles/pallas_call | solution.py:534
  208.8 33.9 %square_tiles.1 = bf16[2,4,512,1024]{3,2,1,0:T(8,128)(2,1)} custom-call(s32[2]{0:T(128)} %pad_add_fusion.place, bf16[4,2,2048,2048]{3,2,1,0:T(8,128)(2,1)} %fused_tiles.1.rows_ref.cols_ref, bf16[4,2,2048,2048]{3,2,1,0:T(8,128)(2,1)} %fused_tiles.1.rows_ref.cols_ref), custom_call_target="tpu_custom_call" | custom-call | flops 34359738368 | bytes 62914560 | tf_op jit(solution)/shard_map/square_tiles/pallas_call | solution.py:586

commit v4 on v3

--- a/solution.py
+++ b/solution.py
@@ -245,12 +245,12 @@
     chip = lax.rem(tm + 2, groups)
     side = lax.rem(col + 1, cols)
     bin_half = bins // 2
+    middle = (row == 1) | (row == 2)
     arrival = [(0, 0), (1, 0), (0, 1), (2, 0), (1, 1), (3, 0), (2, 1), (3, 1)]
 
     def row_at(k):
-        low = lax.rem(lax.rem(row, 2) + k % 2, 2)
-        high = lax.rem(row // 2 + k // 2, 2)
-        return 2 * high + low
+        high = row // 2
+        return (row, row + 1 - 2 * lax.rem(row, 2), 2 - high, 3 - 3 * high)[k]
 
     def block_at(n):
         total = 0
@@ -286,11 +286,20 @@
         pltpu.make_async_copy(piece, piece, piece_recv.at[part or 0, t, block]).wait()
 
     def own_sends():
-        return [send(k - 1, tm, 0, col, {"row": row_at(k)}, source=own_ref) for k in (1, 2, 3)]
+        return [send(0, tm, 0, col, {"row": row_at(1)}, source=own_ref)]
+
+    def relays():
+        over, back = {"row": row_at(2)}, {"row": row_at(1)}
+        return [
+            send(1, tm, 0, col, over, source=own_ref),
+            send(2, tm, 1, col, over),
+            send(3, tm, 2, col, back),
+            send(4, tm, 3, col, back),
+        ]
 
     def spread(k):
         source = own_ref if k == 0 else None
-        base = 3 + 8 * k
+        base = 5 + 8 * k
         return [
             send(base, tm, k, col, {"tm": chip}, source=source),
             send(base + 1, tm, k, col, {"col": side}, source=source),
@@ -298,28 +307,34 @@
         ]
 
     def pass_chip(k):
-        base = 6 + 8 * k
+        base = 8 + 8 * k
         return [
             send(base, chip, k, col, {"col": side}, 0),
             send(base + 1, chip, k, col, {"tm": partner}),
         ]
 
     def pass_side(k):
-        base = 8 + 8 * k
+        base = 10 + 8 * k
         return [
             send(base, tm, k, side, {"tm": chip}, 1),
             send(base + 1, tm, k, side, {"tm": partner}),
         ]
 
     def pass_corner(k):
-        return [send(10 + 8 * k, chip, k, side, {"tm": partner})]
+        return [send(12 + 8 * k, chip, k, side, {"tm": partner})]
 
     def start(copies):
         for one in copies:
             one.start()
 
+    def relay(k):
+        @pl.when(middle)
+        def _():
+            relays()[k].start()
+
     def row_piece(k):
         arrive(tm, k, col)
+        relay(k)
         start(spread(k))
 
     def edge_pieces(k):
@@ -347,14 +362,13 @@
         for friend in friends:
             pl.semaphore_signal(barrier, inc=1, device_id=friend, device_id_type=mesh_id)
         pl.semaphore_wait(barrier, len(friends))
-        first, second, third = own_sends()
-        first.start()
+        start(own_sends())
+        relay(0)
         start(spread(0))
-        second.start()
         mine.start()
         row_piece(1)
-        third.start()
         edge_pieces(0)
+        row_piece(2)
         mine.wait()
         edge_pieces(1)
         from_core(0, col)
@@ -362,13 +376,12 @@
 
     @pl.when(step == 1)
     def _():
-        row_piece(2)
         corner_piece(0)
+        row_piece(3)
         from_core(0, side)
 
     @pl.when(step == 3)
     def _():
-        row_piece(3)
         edge_pieces(2)
         from_core(2, col)
 
@@ -433,27 +446,24 @@
         tn, tk = pair(at, who)
         return tn != tk
 
-    @pl.when((step < count) & ((step == 0) | (n != pair(before, core)[0])))
-    def _():
-        @pl.loop(0, bins)
-        def _(g):
-            block = held[:, a, g]
-            crossed = jnp.concatenate([-block[:, rec:], block[:, :rec]], axis=1)
-            left[g, :BLOCK] = block.reshape(deep, BLOCK).T
-            left[g, BLOCK:] = crossed.reshape(deep, BLOCK).T
-
     @pl.when(step >= 3)
     def _():
         @pl.when(turned(step - 3, core))
         def _():
             finish(step - 3, 1)
 
+    def load(g):
+        left[g] = held[:, a, g].reshape(deep, BLOCK).T
+
     def gram_of(g):
-        both = jnp.dot(
-            left[g], held[:, b, g].reshape(deep, BLOCK), preferred_element_type=jnp.float32
-        ).astype(jnp.bfloat16)
-        gram[0, g] = both[:BLOCK]
-        gram[1, g] = both[BLOCK:]
+        block = held[:, b, g]
+        crossed = jnp.concatenate([block[:, rec:], -block[:, :rec]], axis=1)
+        right = jnp.concatenate(
+            [block.reshape(deep, BLOCK), crossed.reshape(deep, BLOCK)], axis=1
+        )
+        both = jnp.dot(left[g], right, preferred_element_type=jnp.float32).astype(jnp.bfloat16)
+        gram[0, g] = both[:, :BLOCK]
+        gram[1, g] = both[:, BLOCK:]
 
     def turn(f):
         mirror[old, f, 0] = tile[old, f, 0].T
@@ -461,7 +471,22 @@
 
     per = bins // (2 * here)
 
-    @pl.when(step < count)
+    fresh = (step == 0) | (n != pair(before, core)[0])
+
+    @pl.when((step < count) & fresh)
+    def _():
+        for k in range(per):
+            load(k)
+
+        @pl.loop(0, 2 * here)
+        def _(f):
+            for k in range(per):
+                gram_of(f * per + k)
+            turn(f)
+            for k in range(per):
+                load(lax.rem(f + 1, 2 * here) * per + k)
+
+    @pl.when((step < count) & jnp.logical_not(fresh))
     def _():
         @pl.loop(0, 2 * here)
         def _(f):
@@ -520,6 +545,12 @@
 
         for one in own_sends():
             one.wait_send()
+
+        @pl.when(middle)
+        def _():
+            for one in relays():
+                one.wait_send()
+
         for k in range(bands):
             for one in spread(k) + pass_chip(k) + pass_side(k) + pass_corner(k):
                 one.wait_send()
@@ -546,12 +577,12 @@
             out_specs=pl.BlockSpec(memory_space=pl.ANY),
             scratch_shapes=[
                 pltpu.VMEM((groups, blocks) + own.shape, jnp.bfloat16),
-                pltpu.VMEM((bins, 2 * BLOCK, groups * both), jnp.bfloat16),
+                pltpu.VMEM((bins, BLOCK, groups * both), jnp.bfloat16),
                 pltpu.VMEM((2, bins, BLOCK, BLOCK), jnp.bfloat16),
                 pltpu.VMEM((2, 2 * here, 2, BLOCK, BLOCK), jnp.bfloat16),
                 pltpu.VMEM((2, 2 * here, 2, BLOCK, BLOCK), jnp.bfloat16),
                 pltpu.SemaphoreType.DMA,
-                pltpu.SemaphoreType.DMA((3 + 8 * bands,)),
+                pltpu.SemaphoreType.DMA((5 + 8 * bands,)),
                 pltpu.SemaphoreType.DMA((2, groups, blocks)),
                 pltpu.SemaphoreType.DMA((2, 2)),
                 pltpu.SemaphoreType.DMA((2, 2)),

time: 243 us -> 220 us (0.905)
  Pallas kernels: 238 us -> 215 us
    pallas_call x1, Pallas kernels: 204 us -> 181 us  [fused_tiles(): pl.pallas_call(functools.partial(fused_kernel, groups, bands, cols, bins,...]
where the time goes in v4:
time: 220 us
  Pallas kernels  215 us (98%)
  local copies, waits for them, and re-layouts  3.87 us (2%)
    pallas_call x1, Pallas kernels, fused_tiles(): pl.pallas_call(functools.partial(fused_kernel, groups, bands, cols, bins,...  181 us
    pallas_call x1, Pallas kernels, square_tiles(): pl.pallas_call(functools.partial(square_kernel, scale), out_shape=jax.Sha...  33.9 us

profile of v4, /device:TPU:0, one launch (start us, length us, event | category | flops | bytes accessed | tf_op | source)
XLA Modules:
  0.0 220.0 jit_solution(8647819606898924704)
XLA Ops:
  0.0 0.6 pad_add_fusion.place
  0.6 0.8 copy.4
  1.3 0.7 add_select_fusion
  2.0 0.7 reshape.6.shift
  2.7 2.4 %copy.5 = bf16[16,2,48,256]{3,2,1,0:T(8,128)(2,1)} copy(bf16[16,2,48,256]{3,0,1,2:T(8,128)(2,1)} %bitcast.10) | data formatting | bytes 1572864 | tf_op jit(solution)/shard_map/transpose | solution.py:645
  5.1 180.9 %fused_tiles.1.rows_ref.cols_ref = bf16[4,2,2048,2048]{3,2,1,0:T(8,128)(2,1)} custom-call(s32[64]{0:T(128)} %reshape.6.shift, bf16[16,96,256]{2,1,0:T(8,128)(2,1)} %bitcast.11, bf16[2,4,128,256]{3,2,1,0:T(8,128)(2,1)} %constant.25.clone.kmat_ref), custom_call_target="tpu_custom_call" | custom-call | flops 38654705664 | bytes 104857600 | tf_op jit(solution)/shard_map/fused_tiles/pallas_call | solution.py:565
  186.1 33.9 %square_tiles.1 = bf16[2,4,512,1024]{3,2,1,0:T(8,128)(2,1)} custom-call(s32[2]{0:T(128)} %pad_add_fusion.place, bf16[4,2,2048,2048]{3,2,1,0:T(8,128)(2,1)} %fused_tiles.1.rows_ref.cols_ref, bf16[4,2,2048,2048]{3,2,1,0:T(8,128)(2,1)} %fused_tiles.1.rows_ref.cols_ref), custom_call_target="tpu_custom_call" | custom-call | flops 34359738368 | bytes 62914560 | tf_op jit(solution)/shard_map/square_tiles/pallas_call | solution.py:617

commit v5 on v4

--- a/solution.py
+++ b/solution.py
@@ -475,24 +475,26 @@
 
     @pl.when((step < count) & fresh)
     def _():
-        for k in range(per):
+        for k in range(2 * per):
             load(k)
 
-        @pl.loop(0, 2 * here)
+        @pl.loop(0, here)
         def _(f):
-            for k in range(per):
-                gram_of(f * per + k)
-            turn(f)
-            for k in range(per):
-                load(lax.rem(f + 1, 2 * here) * per + k)
+            for k in range(2 * per):
+                gram_of(f * 2 * per + k)
+            turn(2 * f)
+            turn(2 * f + 1)
+            for k in range(2 * per):
+                load(lax.rem(f + 1, here) * 2 * per + k)
 
     @pl.when((step < count) & jnp.logical_not(fresh))
     def _():
-        @pl.loop(0, 2 * here)
+        @pl.loop(0, here)
         def _(f):
-            for k in range(per):
-                gram_of(f * per + k)
-            turn(f)
+            for k in range(2 * per):
+                gram_of(f * 2 * per + k)
+            turn(2 * f)
+            turn(2 * f + 1)
 
     @pl.when(step == count)
     def _():
@@ -514,10 +516,10 @@
     def _():
         kernel = kmat_ref[0, shift[a * blocks + b]]
 
-        @pl.loop(0, BLOCK // SUB // 4)
-        def _(quad):
-            for k in range(4):
-                rows = pl.ds(pl.multiple_of((quad * 4 + k) * SUB, SUB), SUB)
+        @pl.loop(0, BLOCK // SUB // 8)
+        def _(part_of):
+            for k in range(8):
+                rows = pl.ds(pl.multiple_of((part_of * 8 + k) * SUB, SUB), SUB)
                 for c in range(2):
                     part = gram[c, :, rows, :].reshape(bins * SUB, BLOCK)
                     mixed = jnp.dot(kernel, part, preferred_element_type=jnp.float32)

time: 220 us -> 204 us (0.927)
  Pallas kernels: 215 us -> 198 us
    pallas_call x1, Pallas kernels: 181 us -> 165 us  [fused_tiles(): pl.pallas_call(functools.partial(fused_kernel, groups, bands, cols, bins,...]
where the time goes in v5:
time: 204 us
  Pallas kernels  198 us (97%)
  local copies, waits for them, and re-layouts  3.87 us (2%)
    pallas_call x1, Pallas kernels, fused_tiles(): pl.pallas_call(functools.partial(fused_kernel, groups, bands, cols, bins,...  165 us
    pallas_call x1, Pallas kernels, square_tiles(): pl.pallas_call(functools.partial(square_kernel, scale), out_shape=jax.Sha...  33.9 us

profile of v5, /device:TPU:0, one launch (start us, length us, event | category | flops | bytes accessed | tf_op | source)
XLA Modules:
  0.0 203.6 jit_solution(6328233759871343602)
XLA Ops:
  0.0 0.6 pad_add_fusion.place
  0.6 0.8 copy.4
  1.3 0.7 add_select_fusion
  2.0 0.7 reshape.6.shift
  2.7 2.4 %copy.5 = bf16[16,2,48,256]{3,2,1,0:T(8,128)(2,1)} copy(bf16[16,2,48,256]{3,0,1,2:T(8,128)(2,1)} %bitcast.10) | data formatting | bytes 1572864 | tf_op jit(solution)/shard_map/transpose | solution.py:647
  5.1 164.5 %fused_tiles.1.rows_ref.cols_ref = bf16[4,2,2048,2048]{3,2,1,0:T(8,128)(2,1)} custom-call(s32[64]{0:T(128)} %reshape.6.shift, bf16[16,96,256]{2,1,0:T(8,128)(2,1)} %bitcast.11, bf16[2,4,128,256]{3,2,1,0:T(8,128)(2,1)} %constant.25.clone.kmat_ref), custom_call_target="tpu_custom_call" | custom-call | flops 38654705664 | bytes 104857600 | tf_op jit(solution)/shard_map/fused_tiles/pallas_call | solution.py:567
  169.7 33.9 %square_tiles.1 = bf16[2,4,512,1024]{3,2,1,0:T(8,128)(2,1)} custom-call(s32[2]{0:T(128)} %pad_add_fusion.place, bf16[4,2,2048,2048]{3,2,1,0:T(8,128)(2,1)} %fused_tiles.1.rows_ref.cols_ref, bf16[4,2,2048,2048]{3,2,1,0:T(8,128)(2,1)} %fused_tiles.1.rows_ref.cols_ref), custom_call_target="tpu_custom_call" | custom-call | flops 34359738368 | bytes 62914560 | tf_op jit(solution)/shard_map/square_tiles/pallas_call | solution.py:619

commit v6 on v4

--- a/solution.py
+++ b/solution.py
@@ -469,30 +469,30 @@
         mirror[old, f, 0] = tile[old, f, 0].T
         mirror[old, f, 1] = -tile[old, f, 1].T
 
-    per = bins // (2 * here)
-
     fresh = (step == 0) | (n != pair(before, core)[0])
 
     @pl.when((step < count) & fresh)
     def _():
-        for k in range(per):
+        for k in range(bins // 2):
             load(k)
 
-        @pl.loop(0, 2 * here)
-        def _(f):
-            for k in range(per):
-                gram_of(f * per + k)
-            turn(f)
-            for k in range(per):
-                load(lax.rem(f + 1, 2 * here) * per + k)
+        @pl.loop(0, 2)
+        def _(part_of):
+            for k in range(bins // 2):
+                gram_of(part_of * (bins // 2) + k)
+            for k in range(here):
+                turn(part_of * here + k)
+            for k in range(bins // 2):
+                load((1 - part_of) * (bins // 2) + k)
 
     @pl.when((step < count) & jnp.logical_not(fresh))
     def _():
-        @pl.loop(0, 2 * here)
-        def _(f):
-            for k in range(per):
-                gram_of(f * per + k)
-            turn(f)
+        @pl.loop(0, 2)
+        def _(part_of):
+            for k in range(bins // 2):
+                gram_of(part_of * (bins // 2) + k)
+            for k in range(here):
+                turn(part_of * here + k)
 
     @pl.when(step == count)
     def _():
@@ -514,16 +514,14 @@
     def _():
         kernel = kmat_ref[0, shift[a * blocks + b]]
 
-        @pl.loop(0, BLOCK // SUB // 4)
-        def _(quad):
-            for k in range(4):
-                rows = pl.ds(pl.multiple_of((quad * 4 + k) * SUB, SUB), SUB)
-                for c in range(2):
-                    part = gram[c, :, rows, :].reshape(bins * SUB, BLOCK)
-                    mixed = jnp.dot(kernel, part, preferred_element_type=jnp.float32)
-                    tile[slot, :, c, rows, :] = mixed.astype(jnp.bfloat16).reshape(
-                        2 * here, SUB, BLOCK
-                    )
+        for k in range(BLOCK // SUB):
+            rows = pl.ds(k * SUB, SUB)
+            for c in range(2):
+                part = gram[c, :, rows, :].reshape(bins * SUB, BLOCK)
+                mixed = jnp.dot(kernel, part, preferred_element_type=jnp.float32)
+                tile[slot, :, c, rows, :] = mixed.astype(jnp.bfloat16).reshape(
+                    2 * here, SUB, BLOCK
+                )
 
         begin(step, 0)
 

time: 220 us -> 197 us (0.90)
  Pallas kernels: 215 us -> 192 us
    pallas_call x1, Pallas kernels: 181 us -> 158 us  [fused_tiles(): pl.pallas_call(functools.partial(fused_kernel, groups, bands, cols, bins,...]
where the time goes in v6:
time: 197 us
  Pallas kernels  192 us (97%)
  local copies, waits for them, and re-layouts  3.87 us (2%)
    pallas_call x1, Pallas kernels, fused_tiles(): pl.pallas_call(functools.partial(fused_kernel, groups, bands, cols, bins,...  158 us
    pallas_call x1, Pallas kernels, square_tiles(): pl.pallas_call(functools.partial(square_kernel, scale), out_shape=jax.Sha...  33.9 us

profile of v6, /device:TPU:0, one launch (start us, length us, event | category | flops | bytes accessed | tf_op | source)
XLA Modules:
  0.0 196.9 jit_solution(9244629874136571639)
XLA Ops:
  0.0 0.6 pad_add_fusion.place
  0.6 0.8 copy.4
  1.3 0.7 add_select_fusion
  2.0 0.7 reshape.6.shift
  2.7 2.4 %copy.5 = bf16[16,2,48,256]{3,2,1,0:T(8,128)(2,1)} copy(bf16[16,2,48,256]{3,0,1,2:T(8,128)(2,1)} %bitcast.10) | data formatting | bytes 1572864 | tf_op jit(solution)/shard_map/transpose | solution.py:643
  5.1 157.8 %fused_tiles.1.rows_ref.cols_ref = bf16[4,2,2048,2048]{3,2,1,0:T(8,128)(2,1)} custom-call(s32[64]{0:T(128)} %reshape.6.shift, bf16[16,96,256]{2,1,0:T(8,128)(2,1)} %bitcast.11, bf16[2,4,128,256]{3,2,1,0:T(8,128)(2,1)} %constant.25.clone.kmat_ref), custom_call_target="tpu_custom_call" | custom-call | flops 38654705664 | bytes 104857600 | tf_op jit(solution)/shard_map/fused_tiles/pallas_call | solution.py:563
  163.0 33.9 %square_tiles.1 = bf16[2,4,512,1024]{3,2,1,0:T(8,128)(2,1)} custom-call(s32[2]{0:T(128)} %pad_add_fusion.place, bf16[4,2,2048,2048]{3,2,1,0:T(8,128)(2,1)} %fused_tiles.1.rows_ref.cols_ref, bf16[4,2,2048,2048]{3,2,1,0:T(8,128)(2,1)} %fused_tiles.1.rows_ref.cols_ref), custom_call_target="tpu_custom_call" | custom-call | flops 34359738368 | bytes 62914560 | tf_op jit(solution)/shard_map/square_tiles/pallas_call | solution.py:615
